TPU v7x, 32 devices: a whole 2x2x4 slice. The times are simulated.
32 devices in a mesh: orb: 8 (over y, x, core), aux: 4 (over z).
Axes of the slice: x: 2, y: 2, z: 4, core: 2. Of those that a mesh axis runs over, the one named last changes fastest.
Arguments:
- orbital_slabs: float32 [8, 8192, 1024], P('orb', 'aux'), may hold values from -0.625 to 0.625
- occupied_energy: float32 [8], replicated, may hold values from -1.5 to -0.3
- virtual_energy: float32 [1024], replicated, may hold values from 0.3 to 2.5
- virtual_count: int32 [8], replicated, may hold values from 512 to 1024, as said below
Outputs:
- density: float32 [8, 8192, 1024], P('orb', 'aux')
Inputs may be any that keep to these rules, and one draw needn't show every extreme that they name: `virtual_count`: the largest count is 1024 in every draw.
All inputs are finite; a program needn't handle non-finite values.
Results may differ from a plain program's by a relative error of at most 0.0003.
Values sent between devices are 32-bit elements; how exact they have to be, the bound alone decides.
A program may use at most 64 MiB of HBM per device.

v0:
```python
import jax
import jax.numpy as jnp
from jax import lax
from jax.sharding import PartitionSpec as P

highest_mode = lax.Precision.HIGHEST


def from_behind(block, axis, distance):
    devices = range(lax.axis_size(axis))
    route = [((i - distance) % len(devices), i) for i in devices]
    return lax.ppermute(block, axis, route)


def pair_amplitude(
    slab_one, slab_two, occupied_energy, virtual_energy, virtual_count, orbital_one, orbital_two
):
    partial_sum = lax.dot_general(
        slab_one,
        slab_two,
        (((0,), (0,)), ((), ())),
        precision=highest_mode,
        preferred_element_type=jnp.float32,
    )
    virtuals = virtual_energy.shape[0]
    positions = jnp.arange(virtuals, dtype=jnp.int32)
    mask_two = (positions < virtual_count[orbital_two]).astype(jnp.float32)
    pair_energy = occupied_energy[orbital_one] + occupied_energy[orbital_two]
    coupling = lax.psum(partial_sum, "aux")
    mask_one = (positions < virtual_count[orbital_one]).astype(jnp.float32)
    denominator = virtual_energy[:, None] + virtual_energy[None, :] - pair_energy
    return (2.0 * coupling - coupling.T) * mask_one[:, None] * mask_two[None, :] / denominator


def shards(orbital_slabs, occupied_energy, virtual_energy, virtual_count):
    own_slab = orbital_slabs[0]
    groups = lax.axis_size("orb")
    position = lax.axis_index("orb")
    partner = from_behind(own_slab, "orb", -1)
    later = (position + 1) % groups
    amplitude = pair_amplitude(
        own_slab, partner, occupied_energy, virtual_energy, virtual_count, position, later
    )
    density = lax.dot_general(
        partner,
        amplitude,
        (((1,), (1,)), ((), ())),
        precision=highest_mode,
        preferred_element_type=jnp.float32,
    )
    outgoing = jnp.dot(
        own_slab, amplitude, precision=highest_mode, preferred_element_type=jnp.float32
    )
    density = density + from_behind(outgoing, "orb", 1)
    return density[None]


def solution(mesh):
    placed = (P("orb", "aux", None), P(), P(), P())
    return jax.shard_map(
        shards, mesh=mesh, in_specs=placed, out_specs=P("orb", "aux", None), check_vma=False
    )
```

profile of v0, /device:TPU:1, one launch (start us, length us, event | category | flops | bytes accessed | tf_op | source)
XLA Modules:
  0.0 498.5 jit_solution(4438201685957152926)
XLA Ops:
  6.5 0.0 all-reduce.2.cloned.1.call-start
  6.5 0.1 collective-permute-start
  6.6 93.9 %collective-permute-done = f32[2048,1024]{1,0:T(8,128)S(1)} collective-permute-done((f32[2048,1024]{1,0:T(8,128)}, f32[2048,1024]{1,0:T(8,128)S(1)}, u32[]{:S(2)}, u32[]{:S(2)}) %collective-permute-start) | collective-permute-done | bytes 8388640 | tf_op jit(solution)/shard_map/ppermute | solution.py:12
  100.5 0.0 copy-start.4
  100.5 3.2 copy-done.4
  103.7 30.4 %fusion.7 = f32[1024,1024]{1,0:T(8,128)} fusion(f32[2048,1024]{1,0:T(8,128)S(1)} %collective-permute-done, f32[1,2048,1024]{2,1,0:T(8,128)} %param.4), kind=kOutput, calls=%fused_computation.12 | convolution fusion | flops 25769803776 | bytes 20971520 | tf_op jit(solution)/shard_map/dot_general | solution.py:18
  134.0 0.0 copy-start.2
  134.1 0.0 copy-start.3
  134.1 0.0 all-reduce.2.cloned.1.call-update
  134.1 0.6 copy-done.2
  134.7 0.6 fusion.12
  136.6 0.0 copy-done.3
  136.6 0.6 fusion.11
  137.2 1.2 fusion.4
  138.5 0.0 copy-start.5
  138.5 152.3 %all-reduce.2.cloned.1.call-done = f32[1024,1024]{1,0:T(8,128)} async-done(((f32[1024,1024]{1,0:T(8,128)}), f32[1024,1024]{1,0:T(8,128)}) %all-reduce.2.cloned.1.call-update) | async-done | bytes 4194320 | tf_op jit(solution)/shard_map/psum | solution.py:29
  290.8 5.3 %copy.5 = f32[1024,1024]{0,1:T(8,128)} copy(f32[1024,1024]{1,0:T(8,128)} %all-reduce.2.cloned.1.call-done) | data formatting | bytes 8388608 | tf_op jit(solution)/shard_map/psum | solution.py:29
  296.2 0.0 copy-done.5
  296.2 0.0 copy-start
  296.2 0.0 copy-start.1
  296.2 34.9 %convolution_bitcast_fusion = f32[2048,1024]{0,1:T(8,128)} fusion(f32[1,2048,1024]{2,1,0:T(8,128)} %param.4, f32[1024,1024]{1,0:T(8,128)} %all-reduce.2.cloned.1.call-done, f32[1024,1024]{0,1:T(8,128)} %copy.5, f32[]{:T(128)} %bitcast.4, f32[1024]{0:T(1024)S(1)} %copy-done.5, f32[1024]{0:T(1024)S(1)} %get-tuple-element.10, f32[1024]{0:T(1024)S(1)} %get-tuple-element.9), kind=kOutput, calls=%fused_computation.2 | convolution fusion | flops 25777143808 | bytes 25178116 | tf_op jit(solution)/shard_map/dot_general | solution.py:51
  331.0 1.8 collective-permute-start.1
  332.8 90.7 %collective-permute-done.1 = f32[2048,1024]{0,1:T(8,128)S(1)} collective-permute-done((f32[2048,1024]{0,1:T(8,128)}, f32[2048,1024]{0,1:T(8,128)S(1)}, u32[]{:S(2)}, u32[]{:S(2)}) %collective-permute-start.1) | collective-permute-done | bytes 8388640 | tf_op jit(solution)/shard_map/ppermute | solution.py:12
  423.5 0.0 copy-done
  423.5 0.0 copy-done.1
  423.5 58.9 %fusion = f32[1,2048,1024]{1,2,0:T(8,128)} fusion(f32[2048,1024]{0,1:T(8,128)S(1)} %collective-permute-done.1, f32[2048,1024]{1,0:T(8,128)} %copy-done.4, f32[1024,1024]{1,0:T(8,128)S(1)} %copy-done, f32[1024,1024]{0,1:T(8,128)S(1)} %copy-done.1, f32[]{:T(128)} %bitcast.4, f32[1024]{0:T(1024)S(1)} %copy-done.5, f32[1024]{0:T(1024)S(1)} %get-tuple-element.10, ...), kind=kOutput, calls=%fused_computation.1 | convolution fusion | flops 25779240960 | bytes 33566724 | tf_op jit(solution)/shard_map/dot_general | solution.py:44
  482.4 9.2 %copy.6 = f32[1,2048,1024]{2,1,0:T(8,128)} copy(f32[1,2048,1024]{1,2,0:T(8,128)} %fusion) | data formatting | bytes 16777216 | tf_op jit(solution)/shard_map/broadcast_in_dim | solution.py:55
Async XLA Ops:
  6.5 284.3 %all-reduce.2.cloned.1.call-start = ((), (), s32[]{:S(2)}) async-start(), calls=%async_computation | async-start | bytes 8388608 | tf_op jit(solution)/shard_map/psum | solution.py:29
  6.5 93.9 %collective-permute-start = (f32[2048,1024]{1,0:T(8,128)}, f32[2048,1024]{1,0:T(8,128)S(1)}, u32[]{:S(2)}, u32[]{:S(2)}) collective-permute-start(f32[2048,1024]{1,0:T(8,128)} %bitcast.28), channel_id=1, source_target_pairs={{4,0},{8,4},{12,8},{16,12},{20,16},{24,20},{28,24},{0,28},{5,1},{9... | collective-permute-start | bytes 25165832 | tf_op jit(solution)/shard_map/ppermute | solution.py:12
  100.5 3.2 copy-start.4
  134.0 0.7 copy-start.2
  134.1 2.5 copy-start.3
  138.5 157.7 %copy-start.5 = (f32[1024]{0:T(1024)S(1)}, f32[1024]{0:T(1024)}, u32[]{:S(2)}) copy-start(f32[1024]{0:T(1024)} %param.6) | copy-start | bytes 12292
  296.2 127.4 %copy-start = (f32[1024,1024]{1,0:T(8,128)S(1)}, f32[1024,1024]{1,0:T(8,128)}, u32[]{:S(2)}) copy-start(f32[1024,1024]{1,0:T(8,128)} %all-reduce.2.cloned.1.call-done) | copy-start | bytes 12582916
  296.2 127.4 %copy-start.1 = (f32[1024,1024]{0,1:T(8,128)S(1)}, f32[1024,1024]{0,1:T(8,128)}, u32[]{:S(2)}) copy-start(f32[1024,1024]{0,1:T(8,128)} %copy.5) | copy-start | bytes 12582916
  331.0 92.5 %collective-permute-start.1 = (f32[2048,1024]{0,1:T(8,128)}, f32[2048,1024]{0,1:T(8,128)S(1)}, u32[]{:S(2)}, u32[]{:S(2)}) collective-permute-start(f32[2048,1024]{0,1:T(8,128)} %convolution_bitcast_fusion), channel_id=1, source_target_pairs={{28,0},{0,4},{4,8},{8,12},{12,16},{16,20},{20,24},{24,28},{29,1},{... | collective-permute-start | bytes 25165832 | tf_op jit(solution)/shard_map/ppermute | solution.py:12
Sparse Core Ops, SparseCore 0:
  134.2 156.5 all-reduce.1
where the time goes:
time: 501 us; the launch traced here: 499 us
  waiting for transfers between devices  337 us (67%)
  matrix products  124 us (25%)
  local copies, waits for them, and re-layouts  19.7 us (4%)
  between operations  14.7 us (3%)
    ppermute x2, waiting for transfers between devices, from_behind(): return lax.ppermute(block, axis, route)  185 us
    psum x1, waiting for transfers between devices, pair_amplitude(): coupling = lax.psum(partial_sum, 'aux')  152 us
    dot_general x1, matrix products, shards(): lax.dot_general(partner, amplitude, (((1,), (1,)), ((), ())), precision=h...  58.9 us
    dot_general x1, matrix products, shards(): jnp.dot(own_slab, amplitude, precision=highest_mode, preferred_element_ty...  34.9 us
    dot_general x1, matrix products, pair_amplitude(): lax.dot_general(slab_one, slab_two, (((0,), (0,)), ((), ())), precision=h...  30.4 us
  transfers between devices with their start and end apart: 3, of which 3 were waited for; matrix products, arithmetic and copies ran while one was open for 0% of the time, Pallas kernels for 0%

commit v1 on v0

v1 whole, which is shorter than its diff:
```python
import functools

import jax
import jax.numpy as jnp
from jax import lax
from jax.experimental import pallas as pl
from jax.experimental.pallas import tpu as pltpu
from jax.sharding import PartitionSpec as P

MESH = pl.DeviceIdType.MESH
NN = (((1,), (0,)), ((), ()))
NT = (((1,), (1,)), ((), ()))


def halves(x):
    high = x.astype(jnp.bfloat16)
    return high, (x - high.astype(jnp.float32)).astype(jnp.bfloat16)


def dot3(ah, al, bh, bl, dims):
    dot = functools.partial(lax.dot_general, dimension_numbers=dims, preferred_element_type=jnp.float32)
    return dot(ah, bh) + (dot(ah, bl) + dot(al, bh))


def pair_kernel(
    orbs, auxs, chunk, block,
    slab_hbm, mask_one, virt_col, mask_two, virt_row,
    near_hbm, far_hbm,
    own, high, low, partner, part_high, part_low, coupling, prefix, suffix, send_up,
    amp_high, amp_low,
    load_sem, slab_send, slab_recv, right_send, right_recv, left_send, left_recv,
    far_send, far_recv, near_sem,
):
    rows, virtuals = own.shape
    chunks, blocks = virtuals // chunk, rows // block
    o, z = lax.axis_index("orb"), lax.axis_index("aux")
    before, after = lax.rem(o + orbs - 1, orbs), lax.rem(o + 1, orbs)
    first, last = z == 0, z == auxs - 1

    load = pltpu.make_async_copy(slab_hbm, own, load_sem)
    load.start()

    barrier = pltpu.get_barrier_semaphore()
    for there in (before, after):
        pl.semaphore_signal(barrier, inc=1, device_id=(there, z), device_id_type=MESH)

    @pl.when(z > 0)
    def _():
        pl.semaphore_signal(barrier, inc=1, device_id=(o, z - 1), device_id_type=MESH)

    @pl.when(z < auxs - 1)
    def _():
        pl.semaphore_signal(barrier, inc=1, device_id=(o, z + 1), device_id_type=MESH)

    ends = jnp.where(first, 1, 0) + jnp.where(last, 1, 0)
    pl.semaphore_wait(barrier, 4 - ends)

    def slab_copy(c):
        columns = pl.ds(pl.multiple_of(c * chunk, chunk), chunk)
        return pltpu.make_async_remote_copy(
            src_ref=slab_hbm.at[:, columns], dst_ref=partner.at[:, columns],
            send_sem=slab_send.at[c], recv_sem=slab_recv.at[c],
            device_id=(before, z), device_id_type=MESH)

    def right_copy(k):
        return pltpu.make_async_remote_copy(
            src_ref=prefix.at[k], dst_ref=prefix.at[k],
            send_sem=right_send.at[k], recv_sem=right_recv.at[k],
            device_id=(o, lax.rem(z + 1, auxs)), device_id_type=MESH)

    def left_copy(k):
        return pltpu.make_async_remote_copy(
            src_ref=send_up.at[k], dst_ref=suffix.at[k],
            send_sem=left_send.at[k], recv_sem=left_recv.at[k],
            device_id=(o, lax.rem(z + auxs - 1, auxs)), device_id_type=MESH)

    def far_copy(r):
        span = pl.ds(pl.multiple_of(r * block, block), block)
        return pltpu.make_async_remote_copy(
            src_ref=own.at[span], dst_ref=far_hbm.at[span],
            send_sem=far_send.at[r], recv_sem=far_recv.at[r],
            device_id=(after, z), device_id_type=MESH)

    def near_copy(r):
        span = pl.ds(pl.multiple_of(r * block, block), block)
        return pltpu.make_async_copy(partner.at[span], near_hbm.at[span], near_sem.at[r])

    def each(count, body):
        lax.fori_loop(0, count, lambda i, x: (body(i), x)[1], 0)

    each(chunks, lambda c: slab_copy(c).start())

    @pl.when(first)
    def _():
        prefix[...] = jnp.zeros_like(prefix)

    @pl.when(last)
    def _():
        suffix[...] = jnp.zeros_like(suffix)

    load.wait()

    def split_own(r):
        span = pl.ds(pl.multiple_of(r * block, block), block)
        high[span], low[span] = halves(own[span])

    each(blocks, split_own)

    def couple(c):
        slab_copy(c).wait_recv()
        columns = pl.ds(pl.multiple_of(c * chunk, chunk), chunk)

        def turn(r):
            span = pl.ds(pl.multiple_of(r * block, block), block)
            part_high[:, span], part_low[:, span] = halves(partner[span, columns].T)

        each(blocks, turn)

        def tile(t):
            width = pl.ds(pl.multiple_of(t * block, block), block)
            coupling[c, :, width] = dot3(part_high[...], part_low[...], high[:, width], low[:, width], NN)

        each(virtuals // block, tile)

    def step(s):
        @pl.when(s < chunks)
        def _():
            couple(s)

        k = s - z

        @pl.when((k >= 0) & (k < chunks))
        def _():
            @pl.when(z > 0)
            def _():
                right_copy(k).wait_recv()

            prefix[k] = prefix[k] + coupling[k]

            @pl.when(z < auxs - 1)
            def _():
                right_copy(k).start()

        m = s - (auxs - 1 - z)

        @pl.when((m >= 0) & (m < chunks))
        def _():
            @pl.when(z < auxs - 1)
            def _():
                left_copy(m).wait_recv()

            send_up[m] = suffix[m] + coupling[m]

            @pl.when(z > 0)
            def _():
                left_copy(m).start()

    each(chunks + auxs - 1, step)

    @pl.when(z < auxs - 1)
    def _():
        each(chunks, lambda k: right_copy(k).wait_send())

    @pl.when(z > 0)
    def _():
        each(chunks, lambda k: left_copy(k).wait_send())

    def total(k):
        coupling[k] = prefix[k] + suffix[k]

    each(chunks, total)

    def amplitude(k):
        span = pl.ds(pl.multiple_of(k * chunk, chunk), chunk)
        for m in range(chunks):
            columns = pl.ds(m * chunk, chunk)
            straight = coupling[m, :, span].T
            crossed = coupling[k, :, columns]
            value = (2.0 * straight - crossed) * mask_one[span] * mask_two[:, columns]
            value = value / (virt_col[span] + virt_row[:, columns])
            amp_high[span, columns], amp_low[span, columns] = halves(value)

    each(chunks, amplitude)

    def far_term(r):
        span = pl.ds(pl.multiple_of(r * block, block), block)

        def tile(t):
            width = pl.ds(pl.multiple_of(t * block, block), block)
            own[span, width] = dot3(high[span], low[span], amp_high[:, width], amp_low[:, width], NN)

        each(virtuals // block, tile)
        far_copy(r).start()

    each(blocks, far_term)

    def near_term(r):
        span = pl.ds(pl.multiple_of(r * block, block), block)
        part_high_r, part_low_r = halves(partner[span])

        def tile(t):
            width = pl.ds(pl.multiple_of(t * block, block), block)
            own_rows = dot3(part_high_r, part_low_r, amp_high[width], amp_low[width], NT)
            partner[span, width] = own_rows

        each(virtuals // block, tile)
        near_copy(r).start()

    each(blocks, near_term)
    each(chunks, lambda c: slab_copy(c).wait_send())
    each(blocks, lambda r: near_copy(r).wait())
    each(blocks, lambda r: far_copy(r).wait())


def shards(orbital_slabs, occupied_energy, virtual_energy, virtual_count):
    slab = orbital_slabs[0]
    rows, virtuals = slab.shape
    orbs, auxs = lax.axis_size("orb"), lax.axis_size("aux")
    o = lax.axis_index("orb")
    j = (o + 1) % orbs
    positions = jnp.arange(virtuals, dtype=jnp.int32)
    mask_one = (positions < virtual_count[o]).astype(jnp.float32)[:, None]
    mask_two = (positions < virtual_count[j]).astype(jnp.float32)[None, :]
    virt_row = (virtual_energy - (occupied_energy[o] + occupied_energy[j]))[None, :]
    chunk = min(128, virtuals)
    block = min(256, rows)
    chunks, blocks = virtuals // chunk, rows // block
    vmem = pl.BlockSpec(memory_space=pltpu.VMEM)
    hbm = pl.BlockSpec(memory_space=pl.ANY)
    f32, bf16 = jnp.float32, jnp.bfloat16
    dma = pltpu.SemaphoreType.DMA
    near, far = pl.pallas_call(
        functools.partial(pair_kernel, orbs, auxs, chunk, block),
        out_shape=[jax.ShapeDtypeStruct((rows, virtuals), f32)] * 2,
        in_specs=[hbm, vmem, vmem, vmem, vmem],
        out_specs=[hbm, hbm],
        scratch_shapes=[
            pltpu.VMEM((rows, virtuals), f32),
            pltpu.VMEM((rows, virtuals), bf16),
            pltpu.VMEM((rows, virtuals), bf16),
            pltpu.VMEM((rows, virtuals), f32),
            pltpu.VMEM((chunk, rows), bf16),
            pltpu.VMEM((chunk, rows), bf16),
            pltpu.VMEM((chunks, chunk, virtuals), f32),
            pltpu.VMEM((chunks, chunk, virtuals), f32),
            pltpu.VMEM((chunks, chunk, virtuals), f32),
            pltpu.VMEM((chunks, chunk, virtuals), f32),
            pltpu.VMEM((virtuals, virtuals), bf16),
            pltpu.VMEM((virtuals, virtuals), bf16),
            dma, dma((chunks,)), dma((chunks,)), dma((chunks,)), dma((chunks,)),
            dma((chunks,)), dma((chunks,)), dma((blocks,)), dma((blocks,)), dma((blocks,)),
        ],
        cost_estimate=pl.CostEstimate(
            flops=18 * rows * virtuals * virtuals, bytes_accessed=16 * rows * virtuals, transcendentals=0),
        compiler_params=pltpu.CompilerParams(
            collective_id=0, has_side_effects=True, vmem_limit_bytes=58 * 2**20),
    )(slab, mask_one, virtual_energy[:, None], mask_two, virt_row)
    return (near + far)[None]


def solution(mesh):
    placed = (P("orb", "aux", None), P(), P(), P())
    return jax.shard_map(
        shards, mesh=mesh, in_specs=placed, out_specs=P("orb", "aux", None), check_vma=False
    )
```

time: 501 us -> 252 us (0.50)
  waiting for transfers between devices: 337 us -> 0 us
  Pallas kernels: 0 us -> 230 us
  matrix products: 124 us -> 0 us
  local copies, waits for them, and re-layouts: 19.7 us -> 4.41 us
  other arithmetic: 1.25 us -> 16.1 us
  between operations: 14.7 us -> 1.27 us
    pallas_call x0 -> x1, Pallas kernels: none -> 230 us  [shards(): pl.pallas_call(functools.partial(pair_kernel, orbs, auxs, chunk, block),...]
    ppermute x2 -> x0, waiting for transfers between devices: 185 us -> none  [from_behind(): return lax.ppermute(block, axis, route)]
    psum x1 -> x0, waiting for transfers between devices: 152 us -> none  [pair_amplitude(): coupling = lax.psum(partial_sum, 'aux')]
    dot_general x3 -> x0, matrix products: 124 us -> none  [the longest x1 58.9 us: shards(): lax.dot_general(partner, amplitude, (((1,), (1,)), ((), ())), precision=h...]
    broadcast_in_dim x0 -> x1, other arithmetic: none -> 12.2 us  [shards(): return (near + far)[None]]
    broadcast_in_dim x1, local copies, waits for them, and re-layouts: 9.24 us -> 1.71 us  [shards(): virtual_energy[:, None]]
    psum x1 -> x0, local copies, waits for them, and re-layouts: 5.34 us -> none  [pair_amplitude(): coupling = lax.psum(partial_sum, 'aux')]
  transfers between devices with their start and end apart: 3 -> 0, of which waited for: 3 -> 0; matrix products, arithmetic and copies ran while one was open for 0% -> 0% of each run, Pallas kernels for 0% -> 0%
where the time goes in v1:
time: 252 us
  Pallas kernels  230 us (91%)
  other arithmetic  16.1 us (6%)
  local copies, waits for them, and re-layouts  4.41 us (2%)
    pallas_call x1, Pallas kernels, shards(): pl.pallas_call(functools.partial(pair_kernel, orbs, auxs, chunk, block),...  230 us
    broadcast_in_dim x1, other arithmetic, shards(): return (near + far)[None]  12.2 us

profile of v1, /device:TPU:1, one launch (start us, length us, event | category | flops | bytes accessed | tf_op | source)
XLA Modules:
  0.0 251.7 jit_solution(8050152280609069861)
XLA Ops:
  0.0 1.3 fusion.1
  2.6 1.4 fusion.2
  4.0 1.2 compare_convert_fusion.mask_two
  5.2 1.3 broadcast_subtract_fusion
  6.5 1.5 fusion.mask_one
  7.9 1.7 copy.5.virt_col
  9.6 229.9 %shard_map.46 = (f32[2048,1024]{1,0:T(8,128)}, f32[2048,1024]{1,0:T(8,128)}) custom-call(f32[2048,1024]{1,0:T(8,128)} %bitcast.10, f32[1024,1]{1,0:T(8,128)} %fusion.mask_one, f32[1024,1]{1,0:T(8,128)} %copy.5.virt_col, f32[1,1024]{1,0:T(1,128)} %compare_convert_fusion.mask_two, f32[1,1024]{1,0:T(1,128)} %bitcast.9), custom_call_target="tpu_custom_call" | custom-call | flops 38654705664 | bytes 33554432 | tf_op jit(solution)/shard_map/pallas_call | solution.py:232
  239.5 12.2 %add_bitcast_fusion = f32[1,2048,1024]{2,1,0:T(8,128)} fusion(f32[2048,1024]{1,0:T(8,128)} %get-tuple-element.7, f32[2048,1024]{1,0:T(8,128)} %get-tuple-element.8), kind=kLoop, calls=%fused_computation | loop fusion | flops 2097152 | bytes 25165824 | tf_op jit(solution)/shard_map/broadcast_in_dim | solution.py:258

commit v2 on v1

v2 whole, which is shorter than its diff:
```python
import functools

import jax
import jax.numpy as jnp
from jax import lax
from jax.experimental import pallas as pl
from jax.experimental.pallas import tpu as pltpu
from jax.sharding import PartitionSpec as P

MESH = pl.DeviceIdType.MESH
NN = (((1,), (0,)), ((), ()))
NT = (((1,), (1,)), ((), ()))


def halves(x):
    high = x.astype(jnp.bfloat16)
    return high, (x - high.astype(jnp.float32)).astype(jnp.bfloat16)


def dot3(ah, al, bh, bl, dims):
    dot = functools.partial(lax.dot_general, dimension_numbers=dims, preferred_element_type=jnp.float32)
    return dot(ah, bh) + (dot(ah, bl) + dot(al, bh))


def pair_kernel(
    orbs, auxs, chunk, block, strip, piece, ahead,
    slab_hbm, occupied, counts, virt_row,
    near_hbm, far_hbm,
    own, high, low, partner, part_high, part_low, coupling, prefix, suffix, send_up,
    amp_high, amp_low,
    load_sem, slab_send, slab_recv, right_send, right_recv, left_send, left_recv,
    far_send, far_recv, near_sem,
):
    rows, virtuals = own.shape
    chunks, blocks = virtuals // chunk, rows // block
    o, z = lax.axis_index("orb"), lax.axis_index("aux")
    before, after = lax.rem(o + orbs - 1, orbs), lax.rem(o + 1, orbs)
    first, last = z == 0, z == auxs - 1

    load = pltpu.make_async_copy(slab_hbm, own, load_sem)
    load.start()

    barrier = pltpu.get_barrier_semaphore()
    for there in (before, after):
        pl.semaphore_signal(barrier, inc=1, device_id=(there, z), device_id_type=MESH)

    @pl.when(z > 0)
    def _():
        pl.semaphore_signal(barrier, inc=1, device_id=(o, z - 1), device_id_type=MESH)

    @pl.when(z < auxs - 1)
    def _():
        pl.semaphore_signal(barrier, inc=1, device_id=(o, z + 1), device_id_type=MESH)

    ends = jnp.where(first, 1, 0) + jnp.where(last, 1, 0)
    pl.semaphore_wait(barrier, 4 - ends)

    def slab_copy(c):
        columns = pl.ds(pl.multiple_of(c * chunk, chunk), chunk)
        return pltpu.make_async_remote_copy(
            src_ref=slab_hbm.at[:, columns], dst_ref=partner.at[:, columns],
            send_sem=slab_send.at[c], recv_sem=slab_recv.at[c],
            device_id=(before, z), device_id_type=MESH)

    def piece_of(k):
        return pl.ds(pl.multiple_of(k * piece, piece), piece)

    def right_copy(k):
        return pltpu.make_async_remote_copy(
            src_ref=prefix.at[piece_of(k)], dst_ref=prefix.at[piece_of(k)],
            send_sem=right_send.at[k], recv_sem=right_recv.at[k],
            device_id=(o, lax.rem(z + 1, auxs)), device_id_type=MESH)

    def left_copy(k):
        return pltpu.make_async_remote_copy(
            src_ref=send_up.at[piece_of(k)], dst_ref=suffix.at[piece_of(k)],
            send_sem=left_send.at[k], recv_sem=left_recv.at[k],
            device_id=(o, lax.rem(z + auxs - 1, auxs)), device_id_type=MESH)

    def far_copy(r):
        span = pl.ds(pl.multiple_of(r * strip, strip), strip)
        return pltpu.make_async_remote_copy(
            src_ref=own.at[span], dst_ref=far_hbm.at[span],
            send_sem=far_send.at[r], recv_sem=far_recv.at[r],
            device_id=(after, z), device_id_type=MESH)

    def near_copy(r):
        span = pl.ds(pl.multiple_of(r * block, block), block)
        return pltpu.make_async_copy(partner.at[span], near_hbm.at[span], near_sem.at[r])

    def each(count, body):
        lax.fori_loop(0, count, lambda i, x: (body(i), x)[1], 0)

    each(ahead, lambda c: slab_copy(c).start())

    @pl.when(first)
    def _():
        prefix[...] = jnp.zeros_like(prefix)

    @pl.when(last)
    def _():
        suffix[...] = jnp.zeros_like(suffix)

    load.wait()

    def split_own(r):
        span = pl.ds(pl.multiple_of(r * block, block), block)
        high[span], low[span] = halves(own[span])

    each(blocks, split_own)

    def couple(c):
        slab_copy(c).wait_recv()
        columns = pl.ds(pl.multiple_of(c * chunk, chunk), chunk)

        def turn(r):
            span = pl.ds(pl.multiple_of(r * block, block), block)
            part_high[:, span], part_low[:, span] = halves(partner[span, columns].T)

        each(blocks, turn)

        def tile(t):
            width = pl.ds(pl.multiple_of(t * block, block), block)
            coupling[columns, width] = dot3(part_high[...], part_low[...], high[:, width], low[:, width], NN)

        each(virtuals // block, tile)

    count_one, count_two = counts[o], counts[lax.rem(o + 1, orbs)]
    pair_energy = occupied[o] + occupied[lax.rem(o + 1, orbs)]
    square = (chunk, chunk)
    down = lax.broadcasted_iota(jnp.int32, square, 0)
    along = lax.broadcasted_iota(jnp.int32, square, 1)

    def amplitude(k):
        held = pl.ds(pl.multiple_of(k * chunk, chunk), chunk)
        coupling[held] = prefix[held] + suffix[held]
        energy_k = jnp.broadcast_to(virt_row[:, held], square)

        def pair(m):
            other = pl.ds(pl.multiple_of(m * chunk, chunk), chunk)
            gap = energy_k.T + virt_row[:, other] - pair_energy
            at_k, at_m = coupling[held, other], coupling[other, held]
            value = (2.0 * at_m.T - at_k) / gap
            keep = (down + k * chunk < count_one) & (along + m * chunk < count_two)
            amp_high[held, other], amp_low[held, other] = halves(jnp.where(keep, value, 0.0))
            value = (2.0 * at_k.T - at_m) / gap.T
            keep = (down + m * chunk < count_one) & (along + k * chunk < count_two)
            amp_high[other, held], amp_low[other, held] = halves(jnp.where(keep, value, 0.0))

        each(k + 1, pair)

    def right_step(k):
        @pl.when(z > 0)
        def _():
            right_copy(k).wait_recv()

        prefix[piece_of(k)] = prefix[piece_of(k)] + coupling[piece_of(k)]

        @pl.when(z < auxs - 1)
        def _():
            right_copy(k).start()

    def left_step(k):
        @pl.when(z < auxs - 1)
        def _():
            left_copy(k).wait_recv()

        send_up[piece_of(k)] = suffix[piece_of(k)] + coupling[piece_of(k)]

        @pl.when(z > 0)
        def _():
            left_copy(k).start()

    split = chunk // piece

    def step(s):
        @pl.when(s < chunks)
        def _():
            couple(s)

        if ahead < chunks:
            @pl.when(s + ahead < chunks)
            def _():
                slab_copy(s).wait_send()
                slab_copy(s + ahead).start()

        k = s - (z + 1) // 2

        @pl.when((k >= 0) & (k < chunks))
        def _():
            each(split, lambda p: right_step(k * split + p))

        m = s - (auxs - z) // 2

        @pl.when((m >= 0) & (m < chunks))
        def _():
            each(split, lambda p: left_step(m * split + p))

        @pl.when(s >= auxs // 2)
        def _():
            amplitude(s - auxs // 2)

    each(chunks + auxs // 2, step)

    def far_term(r):
        span = pl.ds(pl.multiple_of(r * strip, strip), strip)

        def tile(t):
            width = pl.ds(pl.multiple_of(t * block, block), block)
            own[span, width] = dot3(high[span], low[span], amp_high[:, width], amp_low[:, width], NN)

        each(virtuals // block, tile)
        far_copy(r).start()

    each(rows // strip, far_term)

    def near_term(r):
        span = pl.ds(pl.multiple_of(r * block, block), block)
        part_high_r, part_low_r = halves(partner[span])

        def tile(t):
            width = pl.ds(pl.multiple_of(t * block, block), block)
            own_rows = dot3(part_high_r, part_low_r, amp_high[width], amp_low[width], NT)
            partner[span, width] = own_rows

        each(virtuals // block, tile)
        near_copy(r).start()

    each(blocks, near_term)
    each(ahead, lambda c: slab_copy(chunks - ahead + c).wait_send())

    @pl.when(z < auxs - 1)
    def _():
        each(chunks * split, lambda k: right_copy(k).wait_send())

    @pl.when(z > 0)
    def _():
        each(chunks * split, lambda k: left_copy(k).wait_send())

    each(blocks, lambda r: near_copy(r).wait())
    each(rows // strip, lambda r: far_copy(r).wait())


def add_kernel(near, far, total):
    total[...] = near[...] + far[...]


def chunks_ahead(chunks):
    return chunks


def shards(orbital_slabs, occupied_energy, virtual_energy, virtual_count):
    slab = orbital_slabs[0]
    rows, virtuals = slab.shape
    orbs, auxs = lax.axis_size("orb"), lax.axis_size("aux")
    chunk = min(128, virtuals)
    block = min(256, rows)
    strip = min(128, rows)
    strips = rows // strip
    piece = min(32, chunk)
    ahead = chunks_ahead(virtuals // chunk)
    pieces = virtuals // piece
    chunks, blocks = virtuals // chunk, rows // block
    vmem = pl.BlockSpec(memory_space=pltpu.VMEM)
    smem = pl.BlockSpec(memory_space=pltpu.SMEM)
    hbm = pl.BlockSpec(memory_space=pl.ANY)
    f32, bf16 = jnp.float32, jnp.bfloat16
    dma = pltpu.SemaphoreType.DMA
    near, far = pl.pallas_call(
        functools.partial(pair_kernel, orbs, auxs, chunk, block, strip, piece, ahead),
        out_shape=[jax.ShapeDtypeStruct((rows, virtuals), f32)] * 2,
        in_specs=[hbm, smem, smem, vmem],
        out_specs=[hbm, hbm],
        scratch_shapes=[
            pltpu.VMEM((rows, virtuals), f32),
            pltpu.VMEM((rows, virtuals), bf16),
            pltpu.VMEM((rows, virtuals), bf16),
            pltpu.VMEM((rows, virtuals), f32),
            pltpu.VMEM((chunk, rows), bf16),
            pltpu.VMEM((chunk, rows), bf16),
            pltpu.VMEM((virtuals, virtuals), f32),
            pltpu.VMEM((virtuals, virtuals), f32),
            pltpu.VMEM((virtuals, virtuals), f32),
            pltpu.VMEM((virtuals, virtuals), f32),
            pltpu.VMEM((virtuals, virtuals), bf16),
            pltpu.VMEM((virtuals, virtuals), bf16),
            dma, dma((chunks,)), dma((chunks,)), dma((pieces,)), dma((pieces,)),
            dma((pieces,)), dma((pieces,)), dma((strips,)), dma((strips,)), dma((blocks,)),
        ],
        cost_estimate=pl.CostEstimate(
            flops=18 * rows * virtuals * virtuals, bytes_accessed=16 * rows * virtuals, transcendentals=0),
        compiler_params=pltpu.CompilerParams(
            collective_id=0, has_side_effects=True, vmem_limit_bytes=58 * 2**20),
    )(slab, occupied_energy, virtual_count, virtual_energy[None, :])
    rows_each = pl.BlockSpec((block, virtuals), lambda r: (r, 0))
    return pl.pallas_call(
        add_kernel,
        out_shape=jax.ShapeDtypeStruct((rows, virtuals), f32),
        grid=(blocks,),
        in_specs=[rows_each, rows_each],
        out_specs=rows_each,
        cost_estimate=pl.CostEstimate(
            flops=rows * virtuals, bytes_accessed=12 * rows * virtuals, transcendentals=0),
        compiler_params=pltpu.CompilerParams(vmem_limit_bytes=32 * 2**20),
    )(near, far)[None]


def solution(mesh):
    placed = (P("orb", "aux", None), P(), P(), P())
    return jax.shard_map(
        shards, mesh=mesh, in_specs=placed, out_specs=P("orb", "aux", None), check_vma=False
    )
```

time: 252 us -> 306 us (1.21)
  Pallas kernels: 230 us -> 299 us
  other arithmetic: 16.1 us -> 0 us
    pallas_call x1 -> x2, Pallas kernels: 230 us -> 299 us  [the longest x1 295 us: shards(): pl.pallas_call(functools.partial(pair_kernel, orbs, auxs, chunk, block, s...]
    broadcast_in_dim x1 -> x0, other arithmetic: 12.2 us -> none  [shards(): return (near + far)[None]]
    unnamed x0 -> x4, local copies, waits for them, and re-layouts: none -> 6.76 us
where the time goes in v2:
time: 306 us
  Pallas kernels  299 us (98%)
  local copies, waits for them, and re-layouts  6.76 us (2%)
    pallas_call x1, Pallas kernels, shards(): pl.pallas_call(functools.partial(pair_kernel, orbs, auxs, chunk, block, s...  295 us
    unnamed x4, local copies, waits for them, and re-layouts  6.76 us

profile of v2, /device:TPU:1, one launch (start us, length us, event | category | flops | bytes accessed | tf_op | source)
XLA Modules:
  0.0 306.0 jit_solution(17327978497238309071)
XLA Ops:
  0.0 294.6 %shard_map.46 = (f32[2048,1024]{1,0:T(8,128)}, f32[2048,1024]{1,0:T(8,128)}) custom-call(f32[2048,1024]{1,0:T(8,128)} %bitcast.3, f32[8]{0:T(128)} %occupied.1, s32[8]{0:T(128)} %counts.1, f32[1,1024]{1,0:T(1,128)} %bitcast.4), custom_call_target="tpu_custom_call" | custom-call | flops 38654705664 | bytes 33554432 | tf_op jit(solution)/shard_map/pallas_call | solution.py:269
  294.6 0.0 copy-start
  294.6 3.4 %copy-done = f32[2048,1024]{1,0:T(8,128)S(1)} copy-done((f32[2048,1024]{1,0:T(8,128)S(1)}, f32[2048,1024]{1,0:T(8,128)}, u32[]{:S(2)}) %copy-start) | copy-done | bytes 8388632
  298.0 0.0 copy-start.1
  298.0 3.4 %copy-done.1 = f32[2048,1024]{1,0:T(8,128)S(1)} copy-done((f32[2048,1024]{1,0:T(8,128)S(1)}, f32[2048,1024]{1,0:T(8,128)}, u32[]{:S(2)}) %copy-start.1) | copy-done | bytes 8388632
  301.3 4.6 %shard_map.47 = f32[2048,1024]{1,0:T(8,128)} custom-call(f32[2048,1024]{1,0:T(8,128)S(1)} %copy-done, f32[2048,1024]{1,0:T(8,128)S(1)} %copy-done.1), custom_call_target="tpu_custom_call" | custom-call | flops 2097152 | bytes 25165824 | tf_op jit(solution)/shard_map/pallas_call | solution.py:296
Async XLA Ops:
  294.6 3.4 %copy-start = (f32[2048,1024]{1,0:T(8,128)S(1)}, f32[2048,1024]{1,0:T(8,128)}, u32[]{:S(2)}) copy-start(f32[2048,1024]{1,0:T(8,128)} %get-tuple-element.7.near) | copy-start | bytes 25165828
  298.0 3.4 %copy-start.1 = (f32[2048,1024]{1,0:T(8,128)S(1)}, f32[2048,1024]{1,0:T(8,128)}, u32[]{:S(2)}) copy-start(f32[2048,1024]{1,0:T(8,128)} %get-tuple-element.8.far) | copy-start | bytes 25165828
